TPU v7x, 128 devices: a whole 4x4x4 slice. The times are simulated.
128 devices in a mesh: section: 4 (over y_lo, core), kv: 32 (over y_hi, x, z).
Axes of the slice: x: 4, y: 4 (y_hi: 2, y_lo: 2; y = y_hi * 2 + y_lo), z: 4, core: 2. Of those that a mesh axis runs over, the one named last changes fastest.
Arguments:
- queries: bfloat16 [4, 256, 8192], P('section', 'kv'), may hold values from -20 to 20
- cache_keys: bfloat16 [4, 65536, 1024], P('section', 'kv'), may hold values from -6 to 6
- cache_values: bfloat16 [4, 65536, 1024], P('section', 'kv'), may hold values from -6 to 6
- new_keys: bfloat16 [4, 256, 1024], P('section', 'kv'), may hold values from -6 to 6
- new_values: bfloat16 [4, 256, 1024], P('section', 'kv'), may hold values from -6 to 6
- lengths: int32 [4, 32], P('section', 'kv'), may hold values from 256 to 2048, as said below
- residual: bfloat16 [4, 256, 8192], P('section', 'kv'), may hold values from -6 to 6
Outputs:
- handed: float32 [4, 256, 8192], P('section', 'kv')
- lse: float32 [4, 256, 64], P('section', 'kv')
Inputs may be any that keep to these rules, and one draw needn't show every extreme that they name: `lengths`: in every section at least one kv index has all 2048 slots live.
All inputs are finite; a program needn't handle non-finite values.
Results may differ from a plain program's by a relative error of at most 0.0003.
Values may be sent and summed in bfloat16 or wider, within the bound.
A program may use at most 128 MiB of HBM per device.

v0:
```python
import jax
import jax.numpy as jnp
from jax import lax
from jax.sharding import PartitionSpec as P

HQ = 64
KVH = 8
HD = 128


def passed_along(array, axis, by):
    size = lax.axis_size(axis)
    return lax.ppermute(array, axis, [(i, (i + by) % size) for i in range(size)])


def partial_attention(block_queries, keys, values, valid):
    scale = HD ** (-0.5)
    rows = block_queries.shape[0]
    per_group = HQ // KVH
    query4 = block_queries.reshape(rows, KVH, per_group, HD)
    keys3 = keys.reshape(keys.shape[0], KVH, HD)
    values3 = values.reshape(values.shape[0], KVH, HD)

    def one_group(group):
        group_queries = lax.dynamic_index_in_dim(query4, group, 1, False)
        group_keys = lax.dynamic_index_in_dim(keys3, group, 1, False)
        group_values = lax.dynamic_index_in_dim(values3, group, 1, False)
        scores = (
            jnp.einsum("qhd,kd->hqk", group_queries, group_keys, preferred_element_type=jnp.float32)
            * scale
        )
        scores = jnp.where(valid[None], scores, -1e30)
        top = jnp.max(scores, axis=2, keepdims=True)
        weights = jnp.exp(scores - top)
        total = jnp.sum(weights, axis=2)
        mixed = jnp.einsum(
            "hqk,kd->qhd",
            weights.astype(jnp.bfloat16),
            group_values,
            preferred_element_type=jnp.float32,
        )
        normed = mixed / jnp.transpose(total)[:, :, None]
        return (normed, jnp.transpose(top[:, :, 0] + jnp.log(total)))

    normed, lses = lax.map(one_group, jnp.arange(KVH, dtype=jnp.int32))
    normed = jnp.transpose(normed, (1, 0, 2, 3)).reshape(rows, HQ * HD)
    lses = jnp.transpose(lses, (1, 0, 2)).reshape(rows, HQ)
    return (normed, lses)


def combine_two(first, second):
    out_first, lse_first = first
    out_second, lse_second = second
    peak = jnp.maximum(lse_first, lse_second)
    joint = peak + jnp.log(jnp.exp(lse_first - peak) + jnp.exp(lse_second - peak))
    rows = out_first.shape[0]
    blended = jnp.exp(lse_first - joint)[..., None] * out_first.reshape(rows, HQ, HD)
    blended = blended + jnp.exp(lse_second - joint)[..., None] * out_second.reshape(rows, HQ, HD)
    return (blended.reshape(rows, HQ * HD), joint)


def per_device(queries, cache_keys, cache_values, new_keys, new_values, lengths, residual):
    scale = HD ** (-0.5)
    rows = queries.shape[1]
    per_group = HQ // KVH
    own_index = lax.axis_index("kv")
    whole = lax.all_gather(queries[0], "kv", axis=0, tiled=True)
    slots = cache_keys.shape[1]
    valid = (jnp.arange(slots) < lengths[0, 0])[None, :]
    parts, part_lses = partial_attention(whole, cache_keys[0], cache_values[0], valid)
    own4 = queries[0].reshape(rows, KVH, per_group, HD)
    query_pos = own_index * rows + jnp.arange(rows)
    start_top = jnp.full((rows, KVH, per_group), -1e30, jnp.float32)
    piece = (
        lax.all_gather(new_keys[0], "kv", axis=0, tiled=True),
        lax.all_gather(new_values[0], "kv", axis=0, tiled=True),
    )
    top = start_top
    piece_keys = piece[0].reshape(piece[0].shape[0], KVH, HD)
    piece_values = piece[1].reshape(piece[1].shape[0], KVH, HD)
    scores = (
        jnp.einsum("qghd,kgd->qghk", own4, piece_keys, preferred_element_type=jnp.float32) * scale
    )
    key_pos = jnp.arange(piece_keys.shape[0])
    allowed = (key_pos[None, :] <= query_pos[:, None])[:, None, None, :]
    scores = jnp.where(allowed, scores, -1e30)
    new_top = jnp.maximum(top, jnp.max(scores, axis=3))
    weights = jnp.where(allowed, jnp.exp(scores - new_top[..., None]), 0.0)
    total = jnp.sum(weights, axis=3)
    added = jnp.einsum(
        "qghk,kgd->qghd",
        weights.astype(jnp.bfloat16),
        piece_values,
        preferred_element_type=jnp.float32,
    )
    accum = added
    accum, top, total = (accum, new_top, total)
    own_part = (accum / total[..., None]).reshape(rows, HQ * HD)
    own_lse = (top + jnp.log(total)).reshape(rows, HQ)
    all_rows = parts.shape[0]
    peak_all = lax.pmax(part_lses.astype(jnp.bfloat16), "kv").astype(part_lses.dtype)
    share = jnp.exp(part_lses - peak_all)
    weighted = (share[..., None] * parts.reshape(all_rows, HQ, HD)).reshape(all_rows, HQ * HD)
    numer, denom = (
        lax.psum_scatter(weighted, "kv", scatter_dimension=0, tiled=True),
        lax.psum_scatter(share, "kv", scatter_dimension=0, tiled=True),
    )
    mine_peak = lax.dynamic_slice_in_dim(peak_all, own_index * rows, rows, 0)
    mine = (numer.reshape(rows, HQ, HD) / denom[..., None]).reshape(rows, HQ * HD)
    mine_lse = mine_peak + jnp.log(denom)
    attn, joint = combine_two((mine, mine_lse), (own_part, own_lse))
    updated = residual[0].astype(jnp.float32) + attn
    handed = passed_along(updated[None], "section", 1)
    return (handed, joint[None])


def solution(mesh):
    return jax.shard_map(
        per_device,
        mesh=mesh,
        in_specs=(
            P("section", "kv", None),
            P("section", "kv", None),
            P("section", "kv", None),
            P("section", "kv", None),
            P("section", "kv", None),
            P("section", "kv"),
            P("section", "kv", None),
        ),
        out_specs=(P("section", "kv", None), P("section", "kv", None)),
        check_vma=False,
    )
```

profile of v0, /device:TPU:1, one launch (start us, length us, event | category | flops | bytes accessed | tf_op | source)
XLA Modules:
  0.0 956.9 jit_solution(3364955438565212292)
XLA Ops:
  7.2 0.7 all-gather.5.cloned.1.call-update
  8.0 6.5 copy.73
  14.5 6.5 copy.72
  20.9 73.4 %all-gather.5.cloned.1.call-done = bf16[1,256,8192]{2,1,0:T(8,128)(2,1)} async-done(((bf16[1,8,8192]{2,1,0:T(8,128)(2,1)}), bf16[1,256,8192]{2,1,0:T(8,128)(2,1)}) %all-gather.5.cloned.1.call-update) | async-done | bytes 4194320 | tf_op jit(solution)/shard_map/all_gather | solution.py:67
  94.4 6.4 copy.74
  100.8 144.0 %while.13 = (s32[]{:T(128)}, f32[8,256,8,128]{1,3,2,0:T(8,128)}, f32[8,256,8]{1,2,0:T(8,128)S(1)}, s32[8]{0:T(128)S(1)}, bf16[2048,8,128]{0,2,1:T(8,128)(2,1)}, ...) while((s32[]{:T(128)}, f32[8,256,8,128]{1,3,2,0:T(8,128)}, ...), condition=%wide.region_3.4_spmd.clone, body=%wide.region_0.3_spmd.clone.sunk | while | flops 2193883136 | bytes 53028020 | solution.py:45
  100.8 0.6 dynamic_slice.52
  103.3 0.7 iota_compare_fusion.3
  104.0 4.1 bitcast_reduce_fusion.2
  108.0 4.5 fusion.48
  112.5 6.2 bitcast_dynamic-update-slice_fusion.4
  118.8 0.6 dynamic_slice.52
  121.3 0.7 iota_compare_fusion.3
  122.0 4.1 bitcast_reduce_fusion.2
  126.0 4.5 fusion.48
  130.5 6.3 bitcast_dynamic-update-slice_fusion.4
  136.8 0.6 dynamic_slice.52
  139.3 0.7 iota_compare_fusion.3
  140.0 4.1 bitcast_reduce_fusion.2
  144.1 4.5 fusion.48
  148.6 6.2 bitcast_dynamic-update-slice_fusion.4
  154.8 0.6 dynamic_slice.52
  157.3 0.7 iota_compare_fusion.3
  158.0 4.1 bitcast_reduce_fusion.2
  162.1 4.5 fusion.48
  166.6 6.2 bitcast_dynamic-update-slice_fusion.4
  172.8 0.6 dynamic_slice.52
  175.3 0.7 iota_compare_fusion.3
  176.0 4.1 bitcast_reduce_fusion.2
  180.1 4.5 fusion.48
  184.6 6.2 bitcast_dynamic-update-slice_fusion.4
  190.8 0.6 dynamic_slice.52
  193.3 0.7 iota_compare_fusion.3
  194.0 4.1 bitcast_reduce_fusion.2
  198.0 4.5 fusion.48
  202.6 6.2 bitcast_dynamic-update-slice_fusion.4
  208.8 0.6 dynamic_slice.52
  211.3 0.7 iota_compare_fusion.3
  212.0 4.1 bitcast_reduce_fusion.2
  216.1 4.5 fusion.48
  220.6 6.2 bitcast_dynamic-update-slice_fusion.4
  226.8 0.6 dynamic_slice.52
  229.3 0.7 iota_compare_fusion.3
  230.0 4.0 bitcast_reduce_fusion.2
  234.1 4.5 fusion.48
  238.6 6.2 bitcast_dynamic-update-slice_fusion.4
  244.8 8.9 copy.96
  253.8 151.5 %pmax.7 = bf16[256,64]{1,0:T(8,128)(2,1)S(1)} all-reduce(bf16[256,64]{1,0:T(8,128)(2,1)S(1)} %convert_element_type.20), channel_id=1, replica_groups=mesh['section'=4,'kv'=32] {'kv'}, use_global_device_ids=true, to_apply=%region_4.5 | all-reduce | flops 16384 | bytes 65536 | tf_op jit(solution)/shard_map/pmax | solution.py:101
  405.3 0.7 copy.79
  406.3 4.6 mul.56
  410.8 17.1 %bitcast_multiply_fusion = f32[256,8192]{1,0:T(8,128)} fusion(f32[256,8192]{1,0:T(8,128)} %copy.96, f32[32,8,64,128]{3,2,1,0:T(8,128)} %bitcast.137), kind=kLoop, calls=%fused_computation.25 | loop fusion | flops 2097152 | bytes 25165824 | tf_op jit(solution)/shard_map/mul | solution.py:103
  427.9 0.7 copy-done.2
  428.6 77.4 %all-gather.1 = bf16[1,256,1024]{2,1,0:T(8,128)(2,1)S(1)} all-gather(bf16[1,8,1024]{2,1,0:T(8,128)(2,1)S(1)} %copy-done.2), channel_id=3, replica_groups=mesh['section'=4,'kv'=32] {'kv'}, dimensions={1}, use_global_device_ids=true | all-gather | bytes 540672 | tf_op jit(solution)/shard_map/all_gather | solution.py:75
  506.3 0.3 fusion.40
  507.0 79.5 %all-gather.2 = bf16[1,256,1024]{2,1,0:T(8,128)(2,1)S(1)} all-gather(bf16[1,8,1024]{2,1,0:T(8,128)(2,1)S(1)} %copy-done.3), channel_id=4, replica_groups=mesh['section'=4,'kv'=32] {'kv'}, dimensions={1}, use_global_device_ids=true | all-gather | bytes 540672 | tf_op jit(solution)/shard_map/all_gather | solution.py:76
  586.7 0.4 fusion.26
  587.1 0.6 dynamic-slice
  588.3 142.4 %all-reduce.3.cloned.1.call-done = f32[256,64]{0,1:T(8,128)} async-done(((f32[256,64]{0,1:T(8,128)}), f32[256,64]{0,1:T(8,128)}) %all-reduce.3.cloned.1.call-update) | async-done | bytes 65552
  730.7 0.8 constant_dynamic-slice_fusion
  731.8 188.2 %reduce-scatter.3.cloned.1.call-done = f32[8,8192]{1,0:T(8,128)} async-done(((f32[256,8192]{1,0:T(8,128)}), f32[8,8192]{1,0:T(8,128)}) %reduce-scatter.3.cloned.1.call-update) | async-done | bytes 262160 | tf_op jit(solution)/shard_map/reduce_scatter | solution.py:105
  920.1 1.2 fusion.32
  921.3 25.0 %collective-permute-start = (f32[1,8,8192]{2,1,0:T(8,128)S(1)}, f32[1,8,8192]{2,1,0:T(8,128)S(1)}, u32[]{:S(2)}, u32[]{:S(2)}) collective-permute-start(f32[1,8,8192]{2,1,0:T(8,128)S(1)} %fusion.32), channel_id=1, source_target_pairs={{0,32},{32,64},{64,96},{96,0},{1,33},{33,65},{65,97},{97,1},{2,34}... | collective-permute-start | bytes 786440 | tf_op jit(solution)/shard_map/ppermute | solution.py:13
  946.3 3.3 collective-permute-done
  949.6 0.7 copy.126
  (46 shorter events, 1.7 us)
Async XLA Ops:
  7.2 87.2 %all-gather.5.cloned.1.call-start = ((), (), s32[]{:S(2)}) async-start(), calls=%async_computation.2 | async-start | bytes 4325376 | tf_op jit(solution)/shard_map/all_gather | solution.py:67
  7.9 722.8 %all-reduce.3.cloned.1.call-start = ((), (), s32[]{:S(2)}) async-start(), calls=%async_computation.3 | async-start | bytes 131072
  406.0 514.0 %reduce-scatter.3.cloned.1.call-start = ((), (), s32[]{:S(2)}) async-start(), calls=%async_computation.1 | async-start | bytes 8650752 | tf_op jit(solution)/shard_map/reduce_scatter | solution.py:105
  427.9 0.7 copy-start.2
  427.9 78.4 %copy-start = (bf16[1,8,8192]{2,1,0:T(8,128)(2,1)S(1)}, bf16[1,8,8192]{2,1,0:T(8,128)(2,1)}, u32[]{:S(2)}) copy-start(bf16[1,8,8192]{2,1,0:T(8,128)(2,1)} %param.9) | copy-start | bytes 393220
  427.9 79.1 %copy-start.3 = (bf16[1,8,1024]{2,1,0:T(8,128)(2,1)S(1)}, bf16[1,8,1024]{2,1,0:T(8,128)(2,1)}, u32[]{:S(2)}) copy-start(bf16[1,8,1024]{2,1,0:T(8,128)(2,1)} %param.13) | copy-start | bytes 49156
  427.9 159.2 %copy-start.5 = (u32[128]{0:T(128)S(1)}, u32[128]{0:T(128)}, u32[]{:S(2)}) copy-start(u32[128]{0:T(128)} %constant.58) | copy-start | bytes 1540
  427.9 492.2 %copy-start.1 = (bf16[1,8,8192]{2,1,0:T(8,128)(2,1)S(1)}, bf16[1,8,8192]{2,1,0:T(8,128)(2,1)}, u32[]{:S(2)}) copy-start(bf16[1,8,8192]{2,1,0:T(8,128)(2,1)} %param.15) | copy-start | bytes 393220
  731.6 218.7 %copy-start.4 = (f32[8,64]{1,0:T(8,128)}, f32[8,64]{1,0:T(8,128)S(1)}, u32[]{:S(2)}) copy-start(f32[8,64]{1,0:T(8,128)S(1)} %get-tuple-element.119) | copy-start | bytes 6148
  921.3 28.4 %collective-permute-start = (f32[1,8,8192]{2,1,0:T(8,128)S(1)}, f32[1,8,8192]{2,1,0:T(8,128)S(1)}, u32[]{:S(2)}, u32[]{:S(2)}) collective-permute-start(f32[1,8,8192]{2,1,0:T(8,128)S(1)} %fusion.32), channel_id=1, source_target_pairs={{0,32},{32,64},{64,96},{96,0},{1,33},{33,65},{65,97},{97,1},{2,34}... | collective-permute-start | bytes 786440 | tf_op jit(solution)/shard_map/ppermute | solution.py:13
Sparse Core Ops, SparseCore 0:
  11.2 83.1 all-gather.4
  406.1 324.5 all-reduce.2
  733.2 186.7 reduce-scatter.2
where the time goes:
time: 959 us; the launch traced here: 957 us
  waiting for transfers between devices  408 us (43%)
  blocking collectives  308 us (32%)
  matrix products  82.9 us (9%)
  other arithmetic  60.1 us (6%)
  local copies, waits for them, and re-layouts  41.9 us (4%)
  starting transfers between devices  25.3 us (3%)
  loops' own time  15.7 us (2%)
  between operations  14.6 us (2%)
    reduce_scatter x1, waiting for transfers between devices, per_device(): lax.psum_scatter(weighted, 'kv', scatter_dimension=0, tiled=True)  188 us
    pmax x1, blocking collectives, per_device(): lax.pmax(part_lses.astype(jnp.bfloat16), 'kv').astype(part_lses.dtype)  151 us
    unnamed x4, waiting for transfers between devices  143 us
    all_gather x1, blocking collectives, per_device(): lax.all_gather(new_values[0], 'kv', axis=0, tiled=True)  79.5 us
    all_gather x1, blocking collectives, per_device(): lax.all_gather(new_keys[0], 'kv', axis=0, tiled=True)  77.4 us
    all_gather x1, waiting for transfers between devices, per_device(): whole = lax.all_gather(queries[0], 'kv', axis=0, tiled=True)  73.4 us
    dot_general x8, matrix products, one_group(): jnp.einsum('hqk,kd->qhd', weights.astype(jnp.bfloat16), group_values, pre...  49.8 us
    reduce_sum x8, other arithmetic, one_group(): total = jnp.sum(weights, axis=2)  36.1 us
  transfers between devices with their start and end apart: 4, of which 4 were waited for; matrix products, arithmetic and copies ran while one was open for 4% of the time, Pallas kernels for 0%

commit v1 on v0

v1 whole, which is shorter than its diff:
```python
import functools

import jax
import jax.numpy as jnp
from jax import lax
from jax.experimental import pallas as pl
from jax.experimental.pallas import tpu as pltpu
from jax.sharding import PartitionSpec as P

MESH = pl.DeviceIdType.MESH
F32, BF16, I16 = jnp.float32, jnp.bfloat16, jnp.int16

HQ, KVH, HD, QB = 64, 8, 128, 8
GH = 4
ROWS = 64
BLK = 80
CTX = 2048
UROWS = 256
NKV = 32
SLOTS = NKV + 4
SCALE = HD**-0.5
LOG2E = 1.4426950408889634
CODE = 32700.0
LOW = -1e30


def kernel(
    len_ref, q_ref, nk_ref, nv_ref, res_ref, k_hbm, v_hbm,
    out_ref, lse_ref,
    ga, kraw, vt, vv, bias, po, pa, bp, ba, rp, rb, ra, resb, rres, lsend, lrecv, notes, inv2, s0, s1, p0, p1, mx,
    kv_sem, g1s, g1r, g2s, g2r, g3s, g3r, u2s, u2r, v2s, v2r, b2s, b2r, rss, rsr, lss, lsr,
):
    s = lax.axis_index("section")
    me = lax.axis_index("kv")
    y, x, z = me // 16, (me // 4) % 4, me % 4
    nxt, prv = (s + 1) % 4, (s + 3) % 4
    here = (me, y * 16 + z * 4 + x)
    along = (x, z)
    within = (z, x)

    def line_pos(yy, a):
        return yy * 16 + a * 4

    def device(half, yy, a, w):
        return yy * 16 + jnp.where(half == 0, a * 4 + w, w * 4 + a)

    def pick(half, pair):
        return jnp.where(half == 0, pair[0], pair[1])

    load_k = pltpu.make_async_copy(k_hbm, kraw, kv_sem.at[0])
    load_v = pltpu.make_async_copy(v_hbm, vv, kv_sem.at[1])
    load_k.start()
    load_v.start()

    bar = pltpu.get_barrier_semaphore()

    def greet(sec, kv):
        pl.semaphore_signal(bar, inc=1, device_id=(sec, kv), device_id_type=MESH)

    for half in range(2):
        for dy in range(2):
            for d in range(4):
                if (dy, d) != (0, 0) and not (half == 1 and d == 0):
                    greet(s, device(half, (y + dy) % 2, along[half], (within[half] + d) % 4))

    def greet_all(i, c):
        greet(prv, i)
        return c

    lax.fori_loop(0, NKV, greet_all, 0)
    greet(nxt, me)

    for half in range(2):
        for gl in range(GH):
            g = half * GH + gl
            for pair in range(4):
                c0 = (g * 8 + pair * 2) * HD
                two = jnp.concatenate(
                    [q_ref[:, c0 : c0 + HD].astype(F32), q_ref[:, c0 + HD : c0 + 2 * HD].astype(F32)], axis=0
                )
                ga[half * NKV + here[half], gl, pair * 16 : pair * 16 + 16, :] = two.astype(BF16)
            cols = slice(g * HD, g * HD + HD)
            two = jnp.concatenate([nk_ref[:, cols].astype(F32), nv_ref[:, cols].astype(F32)], axis=0)
            ga[half * NKV + here[half], gl, ROWS:BLK, :] = two.astype(BF16)
    resb[...] = res_ref[...].astype(F32)

    pl.semaphore_wait(bar, 13 + NKV + 1)

    def send_block(half, dy, d):
        at = ga.at[half * NKV + here[half]]
        pltpu.make_async_remote_copy(
            src_ref=at,
            dst_ref=at,
            send_sem=g1s,
            recv_sem=g1r.at[half, dy],
            device_id=(s, device(half, (y + dy) % 2, along[half], (within[half] + d) % 4)),
            device_id_type=MESH,
        ).start()

    for dy in range(2):
        for d in (1, 3, 2, 0):
            for half in range(2):
                if (dy, d) != (0, 0):
                    send_block(half, dy, d)

    residual = pltpu.make_async_remote_copy(
        src_ref=resb, dst_ref=rres, send_sem=rss, recv_sem=rsr, device_id=(nxt, me), device_id_type=MESH
    )

    slot = lax.broadcasted_iota(jnp.int32, (CTX, HD), 0)
    first = lax.broadcasted_iota(jnp.int32, (CTX, HD), 1) == 0
    bias[...] = jnp.where(first & (slot >= len_ref[0, 0]), LOW, 0.0).astype(BF16)
    load_v.wait()

    def turn(g, c):
        vt[g] = vv[:, pl.ds(pl.multiple_of(g * HD, HD), HD)].T
        return c

    lax.fori_loop(0, KVH, turn, 0)

    def send_line(half, yy, a, to):
        base = half * NKV + line_pos(yy, a)
        copies = (
            (ga.at[pl.ds(base, 4), :, 0:ROWS], g2s, g2r.at[half, yy * 4 + a]),
            (ga.at[pl.ds(base, 4), within[half], ROWS:BLK], g3s, g3r.at[half, yy * 4 + a]),
        )
        for at, send_sem, recv_sem in copies:
            pltpu.make_async_remote_copy(
                src_ref=at,
                dst_ref=at,
                send_sem=send_sem,
                recv_sem=recv_sem,
                device_id=(s, device(half, y, to, within[half])),
                device_id_type=MESH,
            ).start()

    def first_wait(half, dy):
        blocks = ga.at[pl.ds(0, 4 if dy else 3)]
        pltpu.make_async_copy(blocks, blocks, g1r.at[half, dy]).wait()
        yy, a = (y + dy) % 2, along[half]
        send_line(half, yy, a, (a + 1) % 4)
        send_line(half, yy, a, (a + 3) % 4)

    def line_wait(half, yy, a):
        blocks = ga.at[pl.ds(half * NKV + line_pos(yy, a), 4), :, 0:ROWS]
        pltpu.make_async_copy(blocks, blocks, g2r.at[half, yy * 4 + a]).wait()
        blocks = ga.at[pl.ds(half * NKV + line_pos(yy, a), 4), within[half], ROWS:BLK]
        pltpu.make_async_copy(blocks, blocks, g3r.at[half, yy * 4 + a]).wait()

    first_wait(0, 0)
    first_wait(1, 0)

    lane = lax.broadcasted_iota(jnp.int32, (UROWS, HD), 1)

    blank = jnp.zeros((4 * ROWS, HD), BF16)
    lane4 = lane[0 : 4 * ROWS]

    def coded(o):
        r = jnp.maximum(jnp.max(jnp.abs(o), axis=1, keepdims=True), 1e-30)
        inv = pl.reciprocal(r, approx=True) * CODE
        return jnp.round(o * inv).astype(jnp.int32).astype(I16), inv

    def packed(stats):
        total = stats[GH : 2 * GH]
        lse = stats[0:GH] * SCALE + jnp.log(total)
        return jnp.concatenate([lse, 1.0 / (stats[2 * GH : 3 * GH] * total)], axis=0)

    def noted(gl, lanes, m, total, inv, before):
        return jnp.where(
            lanes == gl, m, jnp.where(lanes == GH + gl, total, jnp.where(lanes == 2 * GH + gl, inv, before))
        )

    def send_to(src, dst, send_sem, recv_sem, to):
        pltpu.make_async_remote_copy(
            src_ref=src, dst_ref=dst, send_sem=send_sem, recv_sem=recv_sem, device_id=to, device_id_type=MESH
        ).start()

    def send_block_out(half, base, w, yy, a):
        slot = pick(half, here)
        to = (nxt, device(half, yy, a, w))
        send_to(po.at[base + w], rp.at[half * NKV + slot], u2s, u2r.at[half], to)
        send_to(pa.at[base + w], ra.at[half * SLOTS + slot], b2s, b2r, to)

    def own_block(accs):
        mine = lax.broadcasted_iota(jnp.int32, (8, HD), 0)

        def one(half, c):
            w, a = pick(half, within), pick(half, along)
            base = half * NKV + line_pos(y, a)
            col = lax.broadcasted_iota(jnp.int32, (4 * ROWS, NKV * 16), 1)
            row = lax.broadcasted_iota(jnp.int32, (4 * ROWS, NKV * 16), 0)
            p = col // 16
            src = jnp.where(half == 0, p, (p // 16) * 16 + (p % 4) * 4 + (p // 4) % 4)
            dst = device(half, y, a, row // ROWS)
            allowed = (col % 16 < QB) & (src * QB + col % 16 <= dst * QB + row % QB)
            kv = ga[pl.ds(half * NKV, NKV), w, ROWS:BLK, :].reshape(NKV * 16, HD)
            q = ga[pl.ds(base, 4), w, 0:ROWS, :].reshape(4 * ROWS, HD)
            tiles = [jnp.concatenate([kv[j * 256 : (j + 1) * 256], blank], axis=1) for j in range(2)]
            q = jnp.concatenate([q, blank], axis=1)
            for j in range(2):
                pltpu.matmul_push_rhs(tiles[j], j, 0, transpose=True)
                pltpu.matmul_acc_lhs(accs[j], q, load_staged_rhs=j)
            sc = [pltpu.matmul_pop(accs[j]) for j in range(2)]
            sc = jnp.where(allowed, jnp.concatenate(sc, axis=1), LOW)
            m = jnp.max(sc, axis=1, keepdims=True)
            e = jnp.where(allowed, jnp.exp2((sc - m) * (SCALE * LOG2E)), 0.0)
            total = jnp.sum(e, axis=1, keepdims=True)
            e = pltpu.roll(e, 8, 1).astype(BF16)
            for j in range(2):
                pltpu.matmul_push_rhs(tiles[j], j, 1)
                pltpu.matmul_acc_lhs(accs[2], e[:, j * 256 : (j + 1) * 256], load_staged_rhs=j)
            o = pltpu.matmul_pop(accs[2])[:, 0:HD]
            code, inv = coded(o)
            bp[half] = code.reshape(4, ROWS, HD)
            inv2[...] = noted(w, lane4, m, total, inv, jnp.ones((4 * ROWS, HD), F32))
            for two in range(2):
                flat = packed(inv2[two * 2 * ROWS : (two + 1) * 2 * ROWS, :].T)
                flat = jnp.where(mine % GH == w, flat, jnp.where(mine < GH, LOW, 0.0))
                ba[half, 2 * two] = flat
                ba[half, 2 * two + 1] = pltpu.roll(flat, ROWS, 1)
            for b in range(4):
                to = (nxt, device(half, y, a, b))
                send_to(bp.at[half, b], rb.at[half, w], v2s, v2r.at[half], to)
                send_to(ba.at[half, b], ra.at[half * SLOTS + NKV + w], b2s, b2r, to)
            return c

        lax.fori_loop(0, 2, one, 0)

    def order(t):
        q = t // 2
        dy = jnp.where((q == 1) | (q == 3) | (q == 4) | (q == 7), 1, 0)
        off = jnp.where(q < 2, 0, jnp.where((q == 2) | (q == 4), 3, jnp.where((q == 3) | (q == 5), 1, 2)))
        return t % 2, (y + dy) % 2, off

    def bases_of(t):
        half, yy, off = order(t)
        return (half * NKV + line_pos(yy, (pick(half, along) + off) % 4),)

    def arrived(t):
        half, yy, off = order(t)
        y2 = (y + 1) % 2

        @pl.when(t == 1)
        def _():
            first_wait(0, 1)
            first_wait(1, 1)

        for h in range(2):

            @pl.when((t >= 4) & (half == h))
            def _():
                a = along[h]
                line_wait(h, yy, (a + off) % 4)

                @pl.when(t // 2 == 2)
                def _():
                    send_line(h, y, (a + 3) % 4, (a + 1) % 4)

                @pl.when(t // 2 == 3)
                def _():
                    send_line(h, y2, (a + 1) % 4, (a + 3) % 4)

        @pl.when(t == 10)
        def _():
            residual.start()

    ss, pp = (s0, s1), (p0, p1)
    TILE, CHUNK, STEPS = 256, 32, 8
    ones = jnp.where(lane == 0, 1.0, 0.0).astype(BF16)

    def scores_rhs(bases, gl):
        q = ga[pl.ds(bases[0], 4), gl, 0:ROWS, :].reshape(UROWS, HD)
        pltpu.matmul_push_rhs(jnp.concatenate([q, ones], axis=1), gl % 2, 0, transpose=True)

    def scores_lhs(j, g):
        rows = slice(j * TILE, (j + 1) * TILE)
        return jnp.concatenate([kraw[rows, pl.ds(pl.multiple_of(g * HD, HD), HD)], bias[rows, :]], axis=1)

    def values_push(j, buf):
        pltpu.matmul_push_rhs(pp[buf][j * TILE : (j + 1) * TILE, :], j % 2, 1)

    def values_lhs(j, g):
        return vt[g, :, j * TILE : (j + 1) * TILE]

    def scores_end(j, acc, buf):
        tile = pltpu.matmul_pop(acc)
        ss[buf][j * TILE : (j + 1) * TILE, :] = tile
        high = jnp.max(tile.reshape(TILE // 8, 8, UROWS), axis=0)
        mx[buf] = high if j == 0 else jnp.maximum(mx[buf], high)

    def softmax_chunk(j, m, total, buf):
        rows = slice(j * TILE, (j + 1) * TILE)
        w = jnp.exp2((ss[buf][rows, :] - m) * (SCALE * LOG2E))
        pp[buf][rows, :] = w.astype(BF16)
        added = jnp.sum(w.reshape(TILE // 8, 8, UROWS), axis=0)
        return added if total is None else total + added

    def softmax_end(m, total, gl, turn):
        total = jnp.sum(total, axis=0, keepdims=True)
        notes[turn, gl : gl + 1, :] = m * SCALE + jnp.log(total)
        notes[turn, 2 * GH + gl : 2 * GH + gl + 1, :] = total

    def values_end(o, bases, gl, turn):
        inv = CODE / jnp.maximum(jnp.max(jnp.abs(o), axis=0, keepdims=True), 1e-30)
        code = jnp.round((o * inv).T).astype(jnp.int32).astype(I16)
        po[pl.ds(bases[0], 4), gl] = code.reshape(4, ROWS, HD)
        notes[turn, GH + gl : GH + gl + 1, :] = 1.0 / (inv * notes[turn, 2 * GH + gl : 2 * GH + gl + 1, :])

    def step(accs, after, now, before, pending):
        gl = now[3]
        buf, other = gl % 2, 1 - gl % 2
        score, value = accs[0:2], accs[3 + other]
        g_a, g_b = after[1] * GH + after[3], before[1] * GH + before[3]
        scores_rhs(after[0], after[3])
        values_push(0, other)
        m = total = None
        for j in range(STEPS):
            pltpu.matmul_acc_lhs(score[j % 2], scores_lhs(j, g_a), load_staged_rhs=after[3] % 2 if j == 0 else None)
            pltpu.matmul_acc_lhs(value, values_lhs(j, g_b), load_staged_rhs=j % 2)
            if j == 0:
                for todo in pending:
                    todo()
                m = jnp.max(mx[buf], axis=0, keepdims=True)
            if j + 1 < STEPS:
                values_push(j + 1, other)
            total = softmax_chunk(j, m, total, buf)
            if j > 0:
                scores_end(j - 1, score[(j - 1) % 2], other)
        softmax_end(m, total, gl, now[2])

        def last_tile():
            scores_end(STEPS - 1, score[(STEPS - 1) % 2], other)

        def values():
            values_end(pltpu.matmul_pop(value), before[0], before[3], before[2])

        return last_tile, values

    def pack_notes(bases, turn):
        for pair in range(2):
            flat = notes[turn, 0 : 2 * GH, pair * HD : (pair + 1) * HD]
            pa[bases[0] + 2 * pair] = flat
            pa[bases[0] + 2 * pair + 1] = pltpu.roll(flat, ROWS, 1)

    def send_unit(t):
        half, yy, off = order(t)

        @pl.when(t >= 0)
        def _():
            for w in range(4):
                send_block_out(half, bases_of(t)[0], w, yy, (pick(half, along) + off) % 4)

    def unit(accs, t, c):
        arrived(t)

        @pl.when(t == 15)
        def _():
            own_block(accs)

        tb = jnp.maximum(t - 1, 0)
        new = lambda gl: (bases_of(t), t % 2, t % 2, gl)
        old = lambda gl: (bases_of(tb), tb % 2, (t + 1) % 2, gl)
        todo = step(accs, new(0), old(3), old(2), ())
        todo = step(accs, new(1), new(0), old(3), todo)
        for last in todo:
            last()
        pack_notes(bases_of(tb), (t + 1) % 2)
        send_unit(t - 1)
        todo = step(accs, new(2), new(1), new(0), ())
        todo = step(accs, new(3), new(2), new(1), todo)
        for last in todo:
            last()
        return c

    load_k.wait()
    for ref in (p0, p1):
        ref[...] = jnp.zeros((CTX, UROWS), BF16)
    s1[...] = jnp.zeros((CTX, UROWS), F32)
    mx[...] = jnp.zeros((2, 8, UROWS), F32)
    notes[...] = jnp.ones((2, 16, UROWS), F32)

    def units(*accs):
        lax.fori_loop(0, 16, functools.partial(unit, accs), 0)
        bases, value = bases_of(15), accs[3]
        m, total = jnp.max(mx[1], axis=0, keepdims=True), None
        for j in range(STEPS):
            values_push(j, 0)
            pltpu.matmul_acc_lhs(value, values_lhs(j, 6), load_staged_rhs=j % 2)
            total = softmax_chunk(j, m, total, 1)
        softmax_end(m, total, 3, 1)
        values_end(pltpu.matmul_pop(value), bases, 2, 1)
        for j in range(STEPS):
            values_push(j, 1)
            pltpu.matmul_acc_lhs(value, values_lhs(j, 7), load_staged_rhs=j % 2)
        values_end(pltpu.matmul_pop(value), bases, 3, 1)

    shapes = ((0, UROWS), (0, UROWS), (1, UROWS), (1, HD), (1, HD))
    pl.run_scoped(units, *(pltpu.ACC(one)((size, 2 * HD), F32) for one, size in shapes))
    pack_notes(bases_of(15), 1)
    send_unit(15)

    pltpu.make_async_copy(ra, ra, b2r).wait()
    cols = lax.broadcasted_iota(jnp.int32, (QB, HD), 1)
    lout = jnp.zeros((QB, HD), F32)
    for half in range(2):
        lses = ra[half * SLOTS : (half + 1) * SLOTS, 0:GH, :]
        top = jnp.max(lses, axis=0, keepdims=True)
        lse = top + jnp.log(jnp.sum(jnp.exp(lses - top), axis=0, keepdims=True))
        ra[half * SLOTS : (half + 1) * SLOTS, 0:GH, :] = (
            jnp.exp(lses - lse) * ra[half * SLOTS : (half + 1) * SLOTS, GH : 2 * GH, :]
        )
        flat = jnp.concatenate([lse[0], jnp.zeros((HD - GH, HD), F32)], axis=0).T
        for gl in range(GH):
            for h in range(8):
                piece = flat[h * QB : (h + 1) * QB, gl : gl + 1]
                lout = jnp.where(cols == (half * GH + gl) * 8 + h, piece, lout)
    lsend[...] = lout
    back = pltpu.make_async_remote_copy(
        src_ref=lsend, dst_ref=lrecv, send_sem=lss, recv_sem=lsr, device_id=(prv, me), device_id_type=MESH
    )
    back.start()
    residual.wait_recv()

    for half in range(2):
        parts = rp.at[pl.ds(half * NKV, NKV)]
        pltpu.make_async_copy(parts, parts, u2r.at[half]).wait()
        pltpu.make_async_copy(rb.at[half], rb.at[half], v2r.at[half]).wait()

        def add(n, acc):
            factors = ra[pl.ds(half * SLOTS + n * 16, 16)].reshape(HD, HD).T
            for i in range(16):
                part = rp[half * NKV + n * 16 + i]
                acc = tuple(
                    acc[gl]
                    + part[gl].astype(jnp.int32).astype(F32) * factors[0:ROWS, i * 8 + gl : i * 8 + gl + 1]
                    for gl in range(GH)
                )
            return acc

        acc = lax.fori_loop(0, 2, add, tuple(jnp.zeros((ROWS, HD), F32) for _ in range(GH)))
        rows = ra[half * SLOTS + NKV : (half + 1) * SLOTS].reshape(32, HD)
        factors = jnp.concatenate([rows, jnp.zeros((HD - 32, HD), F32)], axis=0).T
        acc = [
            acc[gl] + rb[half, gl].astype(jnp.int32).astype(F32) * factors[0:ROWS, gl * 9 : gl * 9 + 1]
            for gl in range(GH)
        ]
        for gl in range(GH):
            for h in range(8):
                c0 = ((half * GH + gl) * 8 + h) * HD
                out_ref[:, c0 : c0 + HD] = rres[:, c0 : c0 + HD] + acc[gl][h * QB : (h + 1) * QB, :]

    back.wait_recv()
    lse_ref[...] = lrecv[:, 0:HQ]
    back.wait_send()
    residual.wait_send()
    blocks = ga.at[pl.ds(0, 14)]
    pltpu.make_async_copy(blocks, blocks, g1s).wait()
    blocks = ga.at[pl.ds(0, 48), :, 0:ROWS]
    pltpu.make_async_copy(blocks, blocks, g2s).wait()
    blocks = ga.at[pl.ds(0, 48), 0, ROWS:BLK]
    pltpu.make_async_copy(blocks, blocks, g3s).wait()
    for ref, sem in ((po, u2s), (bp, v2s), (ra, b2s)):
        pltpu.make_async_copy(ref, ref, sem).wait()


def per_device(queries, cache_keys, cache_values, new_keys, new_values, lengths, residual):
    vmem = pl.BlockSpec(memory_space=pltpu.VMEM)
    hbm = pl.BlockSpec(memory_space=pl.ANY)
    dma = pltpu.SemaphoreType.DMA
    handed, lse = pl.pallas_call(
        kernel,
        out_shape=(jax.ShapeDtypeStruct((QB, HQ * HD), F32), jax.ShapeDtypeStruct((QB, HQ), F32)),
        in_specs=[pl.BlockSpec(memory_space=pltpu.SMEM), vmem, vmem, vmem, vmem, hbm, hbm],
        out_specs=(vmem, vmem),
        scratch_shapes=[
            pltpu.VMEM((2 * NKV, GH, BLK, HD), BF16),
            pltpu.VMEM((CTX, KVH * HD), BF16),
            pltpu.VMEM((KVH, HD, CTX), BF16),
            pltpu.VMEM((CTX, KVH * HD), BF16),
            pltpu.VMEM((CTX, HD), BF16),
            pltpu.VMEM((2 * NKV, GH, ROWS, HD), I16),
            pltpu.VMEM((2 * NKV, 8, HD), F32),
            pltpu.VMEM((2, 4, ROWS, HD), I16),
            pltpu.VMEM((2, 4, 8, HD), F32),
            pltpu.VMEM((2 * NKV, GH, ROWS, HD), I16),
            pltpu.VMEM((2, GH, ROWS, HD), I16),
            pltpu.VMEM((2 * SLOTS, 8, HD), F32),
            pltpu.VMEM((QB, HQ * HD), F32),
            pltpu.VMEM((QB, HQ * HD), F32),
            pltpu.VMEM((QB, HD), F32),
            pltpu.VMEM((QB, HD), F32),
            pltpu.VMEM((2, 16, UROWS), F32),
            pltpu.VMEM((4 * ROWS, HD), F32),
            pltpu.VMEM((CTX, UROWS), F32),
            pltpu.VMEM((CTX, UROWS), F32),
            pltpu.VMEM((CTX, UROWS), BF16),
            pltpu.VMEM((CTX, UROWS), BF16),
            pltpu.VMEM((2, 8, UROWS), F32),
            dma((2,)),
            dma,
            dma((2, 2)),
            dma,
            dma((2, 8)),
            dma,
            dma((2, 8)),
            dma,
            dma((2,)),
            dma,
            dma((2,)),
            dma,
            dma,
            dma,
            dma,
            dma,
            dma,
        ],
        compiler_params=pltpu.CompilerParams(
            collective_id=0, has_side_effects=True, vmem_limit_bytes=60 * 1024 * 1024
        ),
        cost_estimate=pl.CostEstimate(
            flops=4 * HQ * 256 * CTX * HD, bytes_accessed=12 * 1024 * 1024, transcendentals=HQ * 256 * CTX
        ),
    )(lengths, queries[0], new_keys[0], new_values[0], residual[0], cache_keys[0], cache_values[0])
    return handed[None], lse[None]


def solution(mesh):
    rows = P("section", "kv", None)
    return jax.shard_map(
        per_device,
        mesh=mesh,
        in_specs=(rows, rows, rows, rows, rows, P("section", "kv"), rows),
        out_specs=(rows, rows),
        check_vma=False,
    )
```

time: 959 us -> 111 us (0.12)
  waiting for transfers between devices: 408 us -> 0 us
  blocking collectives: 308 us -> 0 us
  Pallas kernels: 0 us -> 107 us
  matrix products: 82.9 us -> 0 us
  other arithmetic: 60.1 us -> 0 us
  local copies, waits for them, and re-layouts: 41.9 us -> 2.95 us
  starting transfers between devices: 25.3 us -> 0 us
  loops' own time: 15.7 us -> 0 us
  between operations: 14.6 us -> 1.29 us
    reduce_scatter x1 -> x0, waiting for transfers between devices: 188 us -> none  [per_device(): lax.psum_scatter(weighted, 'kv', scatter_dimension=0, tiled=True)]
    all_gather x2 -> x0, blocking collectives: 157 us -> none  [the longest x1 79.5 us: per_device(): lax.all_gather(new_values[0], 'kv', axis=0, tiled=True)]
    pmax x1 -> x0, blocking collectives: 151 us -> none  [per_device(): lax.pmax(part_lses.astype(jnp.bfloat16), 'kv').astype(part_lses.dtype)]
    unnamed x4 -> x0, waiting for transfers between devices: 143 us -> none
    pallas_call x0 -> x1, Pallas kernels: none -> 107 us  [per_device(): pl.pallas_call(kernel, out_shape=(jax.ShapeDtypeStruct((QB, HQ * HD), F32...]
    dot_general x18 -> x0, matrix products: 82.9 us -> none  [the longest x8 49.8 us: one_group(): jnp.einsum('hqk,kd->qhd', weights.astype(jnp.bfloat16), group_values, pre...]
    all_gather x1 -> x0, waiting for transfers between devices: 73.4 us -> none  [per_device(): whole = lax.all_gather(queries[0], 'kv', axis=0, tiled=True)]
    reduce_sum x9 -> x0, other arithmetic: 36.3 us -> none  [the longest x8 36.1 us: one_group(): total = jnp.sum(weights, axis=2)]
  transfers between devices with their start and end apart: 4 -> 0, of which waited for: 4 -> 0; matrix products, arithmetic and copies ran while one was open for 4% -> 0% of each run, Pallas kernels for 0% -> 0%
where the time goes in v1:
time: 111 us
  Pallas kernels  107 us (96%)
  local copies, waits for them, and re-layouts  2.95 us (3%)
  between operations  1.29 us (1%)
    pallas_call x1, Pallas kernels, per_device(): pl.pallas_call(kernel, out_shape=(jax.ShapeDtypeStruct((QB, HQ * HD), F32...  107 us
    unnamed x2, local copies, waits for them, and re-layouts  2.95 us

profile of v1, /device:TPU:1, one launch (start us, length us, event | category | flops | bytes accessed | tf_op | source)
XLA Modules:
  0.0 111.2 jit_solution(11399323600126523195)
XLA Ops:
  1.3 107.0 %shard_map.86 = (f32[8,8192]{1,0:T(8,128)}, f32[8,64]{1,0:T(8,128)}) custom-call(s32[1,1]{1,0:T(1,128)S(6)} %copy.11.len_ref, bf16[8,8192]{1,0:T(8,128)(2,1)} %bitcast.12, bf16[8,1024]{1,0:T(8,128)(2,1)} %bitcast.14, bf16[8,1024]{1,0:T(8,128)(2,1)} %bitcast.15, bf16[8,8192]{1,0:T(8,128)(2,1)} %bitcast.13, bf16[2048,1024]{1,0:T(8,128)(2,1)} %bitcast.10, ...), custom_call_target="tpu_custom_call" | custom-call | flops 17179869184 | bytes 12582912 | tf_op jit(solution)/shard_map/pallas_call | solution.py:470
  108.3 1.7 %copy.12 = f32[1,8,8192]{2,1,0:T(8,128)} copy(f32[1,8,8192]{2,1,0:T(8,128)} %bitcast.8) | data formatting | bytes 524288
  109.9 1.3 %copy.13 = f32[1,8,64]{2,1,0:T(8,128)} copy(f32[1,8,64]{2,1,0:T(8,128)} %bitcast.9) | data formatting | bytes 4096

commit v2 on v1

--- a/solution.py
+++ b/solution.py
@@ -17,7 +17,7 @@
 CTX = 2048
 UROWS = 256
 NKV = 32
-SLOTS = NKV + 4
+SLOTS = 8
 SCALE = HD**-0.5
 LOG2E = 1.4426950408889634
 CODE = 32700.0
@@ -27,8 +27,8 @@
 def kernel(
     len_ref, q_ref, nk_ref, nv_ref, res_ref, k_hbm, v_hbm,
     out_ref, lse_ref,
-    ga, kraw, vt, vv, bias, po, pa, bp, ba, rp, rb, ra, resb, rres, lsend, lrecv, notes, inv2, s0, s1, p0, p1, mx,
-    kv_sem, g1s, g1r, g2s, g2r, g3s, g3r, u2s, u2r, v2s, v2r, b2s, b2r, rss, rsr, lss, lsr,
+    ga, kraw, vt, vv, bias, po, pa, r1, a1, bp, ba, po2, pa2, rp, ra, resb, rres, lsend, lrecv, notes, inv2, s0, s1, p0, p1, mx,
+    kv_sem, g1s, g1r, g2s, g2r, g3s, g3r, u1s, u1r, b1s, b1r, u2s, u2r, b2s, b2r, rss, rsr, lss, lsr,
 ):
     s = lax.axis_index("section")
     me = lax.axis_index("kv")
@@ -63,11 +63,17 @@
                 if (dy, d) != (0, 0) and not (half == 1 and d == 0):
                     greet(s, device(half, (y + dy) % 2, along[half], (within[half] + d) % 4))
 
-    def greet_all(i, c):
-        greet(prv, i)
-        return c
-
-    lax.fori_loop(0, NKV, greet_all, 0)
+    for half in range(2):
+        for yy in range(2):
+            for w in range(4):
+                if half == 0:
+                    greet(prv, device(0, yy, x, w))
+                else:
+
+                    @pl.when(w != x)
+                    def _():
+                        greet(prv, device(1, yy, z, w))
+
     greet(nxt, me)
 
     for half in range(2):
@@ -84,7 +90,7 @@
             ga[half * NKV + here[half], gl, ROWS:BLK, :] = two.astype(BF16)
     resb[...] = res_ref[...].astype(F32)
 
-    pl.semaphore_wait(bar, 13 + NKV + 1)
+    pl.semaphore_wait(bar, 13 + 14 + 1)
 
     def send_block(half, dy, d):
         at = ga.at[half * NKV + here[half]]
@@ -119,12 +125,11 @@
     lax.fori_loop(0, KVH, turn, 0)
 
     def send_line(half, yy, a, to):
-        base = half * NKV + line_pos(yy, a)
-        copies = (
-            (ga.at[pl.ds(base, 4), :, 0:ROWS], g2s, g2r.at[half, yy * 4 + a]),
-            (ga.at[pl.ds(base, 4), within[half], ROWS:BLK], g3s, g3r.at[half, yy * 4 + a]),
-        )
-        for at, send_sem, recv_sem in copies:
+        blocks = pl.ds(half * NKV + line_pos(yy, a), 4)
+        for at, send_sem, recv_sem in (
+            (ga.at[blocks, :, 0:ROWS], g2s, g2r.at[half, yy * 4 + a]),
+            (ga.at[blocks, within[half], ROWS:BLK], g3s, g3r.at[half, yy * 4 + a]),
+        ):
             pltpu.make_async_remote_copy(
                 src_ref=at,
                 dst_ref=at,
@@ -150,10 +155,9 @@
     first_wait(0, 0)
     first_wait(1, 0)
 
-    lane = lax.broadcasted_iota(jnp.int32, (UROWS, HD), 1)
+    lane = lax.broadcasted_iota(jnp.int32, (4 * ROWS, HD), 1)
 
     blank = jnp.zeros((4 * ROWS, HD), BF16)
-    lane4 = lane[0 : 4 * ROWS]
 
     def coded(o):
         r = jnp.maximum(jnp.max(jnp.abs(o), axis=1, keepdims=True), 1e-30)
@@ -175,33 +179,24 @@
             src_ref=src, dst_ref=dst, send_sem=send_sem, recv_sem=recv_sem, device_id=to, device_id_type=MESH
         ).start()
 
-    def send_block_out(half, base, w, yy, a):
-        slot = pick(half, here)
-        to = (nxt, device(half, yy, a, w))
-        send_to(po.at[base + w], rp.at[half * NKV + slot], u2s, u2r.at[half], to)
-        send_to(pa.at[base + w], ra.at[half * SLOTS + slot], b2s, b2r, to)
-
     def own_block(accs):
-        mine = lax.broadcasted_iota(jnp.int32, (8, HD), 0)
-
         def one(half, c):
-            w, a = pick(half, within), pick(half, along)
-            base = half * NKV + line_pos(y, a)
+            w = pick(half, within)
             col = lax.broadcasted_iota(jnp.int32, (4 * ROWS, NKV * 16), 1)
             row = lax.broadcasted_iota(jnp.int32, (4 * ROWS, NKV * 16), 0)
             p = col // 16
             src = jnp.where(half == 0, p, (p // 16) * 16 + (p % 4) * 4 + (p // 4) % 4)
-            dst = device(half, y, a, row // ROWS)
+            dst = device(half, y, pick(half, along), row // ROWS)
             allowed = (col % 16 < QB) & (src * QB + col % 16 <= dst * QB + row % QB)
             kv = ga[pl.ds(half * NKV, NKV), w, ROWS:BLK, :].reshape(NKV * 16, HD)
-            q = ga[pl.ds(base, 4), w, 0:ROWS, :].reshape(4 * ROWS, HD)
+            q = ga[pl.ds(half * NKV + line_pos(y, pick(half, along)), 4), w, 0:ROWS, :].reshape(4 * ROWS, HD)
             tiles = [jnp.concatenate([kv[j * 256 : (j + 1) * 256], blank], axis=1) for j in range(2)]
             q = jnp.concatenate([q, blank], axis=1)
             for j in range(2):
                 pltpu.matmul_push_rhs(tiles[j], j, 0, transpose=True)
                 pltpu.matmul_acc_lhs(accs[j], q, load_staged_rhs=j)
-            sc = [pltpu.matmul_pop(accs[j]) for j in range(2)]
-            sc = jnp.where(allowed, jnp.concatenate(sc, axis=1), LOW)
+            sc = jnp.concatenate([pltpu.matmul_pop(accs[0]), pltpu.matmul_pop(accs[1])], axis=1)
+            sc = jnp.where(allowed, sc, LOW)
             m = jnp.max(sc, axis=1, keepdims=True)
             e = jnp.where(allowed, jnp.exp2((sc - m) * (SCALE * LOG2E)), 0.0)
             total = jnp.sum(e, axis=1, keepdims=True)
@@ -209,63 +204,108 @@
             for j in range(2):
                 pltpu.matmul_push_rhs(tiles[j], j, 1)
                 pltpu.matmul_acc_lhs(accs[2], e[:, j * 256 : (j + 1) * 256], load_staged_rhs=j)
-            o = pltpu.matmul_pop(accs[2])[:, 0:HD]
-            code, inv = coded(o)
+            code, inv = coded(pltpu.matmul_pop(accs[2])[:, 0:HD])
             bp[half] = code.reshape(4, ROWS, HD)
-            inv2[...] = noted(w, lane4, m, total, inv, jnp.ones((4 * ROWS, HD), F32))
-            for two in range(2):
-                flat = packed(inv2[two * 2 * ROWS : (two + 1) * 2 * ROWS, :].T)
+            inv2[...] = noted(w, lane, m, total, inv, jnp.ones((4 * ROWS, HD), F32))
+            mine = lax.broadcasted_iota(jnp.int32, (8, HD), 0)
+            for pair in range(2):
+                flat = packed(inv2[pair * 2 * ROWS : (pair + 1) * 2 * ROWS, :].T)
                 flat = jnp.where(mine % GH == w, flat, jnp.where(mine < GH, LOW, 0.0))
-                ba[half, 2 * two] = flat
-                ba[half, 2 * two + 1] = pltpu.roll(flat, ROWS, 1)
+                ba[half, 2 * pair] = flat
+                ba[half, 2 * pair + 1] = pltpu.roll(flat, ROWS, 1)
+            return c
+
+        lax.fori_loop(0, 2, one, 0)
+
+    def join(half, dy):
+        yy = (y + dy) % 2
+        a, w = pick(half, along), pick(half, within)
+        line = half * 2 + yy
+        base = half * NKV + line_pos(yy, a)
+        for k in range(3):
+            got = r1.at[line, k]
+            pltpu.make_async_copy(got, got, u1r.at[line, k]).wait()
+            got = a1.at[line, k]
+            pltpu.make_async_copy(got, got, b1r.at[line, k]).wait()
+        notes = [pa[pl.ds(base, 4)]] + [a1[line, k] for k in range(3)] + ([ba[half]] if dy == 0 else [])
+        top = functools.reduce(jnp.maximum, [n[:, 0:GH, :] for n in notes])
+        lse = top + jnp.log(sum(jnp.exp(n[:, 0:GH, :] - top) for n in notes))
+        blank = jnp.zeros((4, GH, HD), F32)
+        factors = [
+            jnp.concatenate([jnp.exp(n[:, 0:GH, :] - lse) * n[:, GH : 2 * GH, :], blank], axis=1).reshape(32, HD)
+            for n in notes
+        ]
+        columns = jnp.concatenate(factors[0:4], axis=0).T
+        if dy == 0:
+            extra = jnp.concatenate([factors[4], jnp.zeros((HD - 32, HD), F32)], axis=0).T
+        inv2[...] = jnp.ones((4 * ROWS, HD), F32)
+        for gl in range(GH):
             for b in range(4):
-                to = (nxt, device(half, y, a, b))
-                send_to(bp.at[half, b], rb.at[half, w], v2s, v2r.at[half], to)
-                send_to(ba.at[half, b], ra.at[half * SLOTS + NKV + w], b2s, b2r, to)
-            return c
-
-        lax.fori_loop(0, 2, one, 0)
+                acc = None
+                for i in range(len(notes)):
+                    if i == 0:
+                        part = po[base + b, gl]
+                    elif i < 4:
+                        part = r1[line, i - 1, b, gl]
+                    else:
+                        part = bp[half, b]
+                    at = (i % 4) * 32 + b * 8 + gl
+                    factor = (columns if i < 4 else extra)[0:ROWS, at : at + 1]
+                    term = part.astype(jnp.int32).astype(F32) * factor
+                    acc = term if acc is None else acc + term
+                code, inv = coded(acc)
+                po2[line, b, gl] = code
+                inv2[b * ROWS : (b + 1) * ROWS, :] = jnp.where(lane[0:ROWS] == gl, inv, inv2[b * ROWS : (b + 1) * ROWS, :])
+        for pair in range(2):
+            scale = 1.0 / inv2[pair * 2 * ROWS : (pair + 1) * 2 * ROWS, :].T[0:GH, :]
+            pa2[line, 2 * pair] = jnp.concatenate([lse[2 * pair], scale], axis=0)
+            pa2[line, 2 * pair + 1] = jnp.concatenate([lse[2 * pair + 1], pltpu.roll(scale, ROWS, 1)], axis=0)
+        for b in range(4):
+            slot = half * SLOTS + y * 4 + w
+            to = (nxt, device(half, yy, a, b))
+            send_to(po2.at[line, b], rp.at[slot], u2s, u2r.at[half], to)
+            send_to(pa2.at[line, b], ra.at[slot], b2s, b2r, to)
 
     def order(t):
         q = t // 2
-        dy = jnp.where((q == 1) | (q == 3) | (q == 4) | (q == 7), 1, 0)
-        off = jnp.where(q < 2, 0, jnp.where((q == 2) | (q == 4), 3, jnp.where((q == 3) | (q == 5), 1, 2)))
+        dy = jnp.where((q == 2) | (q == 3) | (q >= 6), 1, 0)
+        off = jnp.where((q == 0) | (q == 7), 0, jnp.where((q == 1) | (q == 3), 3, jnp.where((q == 2) | (q == 4), 1, 2)))
         return t % 2, (y + dy) % 2, off
 
-    def bases_of(t):
+    def base_of(t):
         half, yy, off = order(t)
-        return (half * NKV + line_pos(yy, (pick(half, along) + off) % 4),)
+        return half * NKV + line_pos(yy, (jnp.where(half == 0, x, z) + off) % 4)
 
     def arrived(t):
         half, yy, off = order(t)
-        y2 = (y + 1) % 2
+        q = t // 2
 
         @pl.when(t == 1)
         def _():
             first_wait(0, 1)
             first_wait(1, 1)
 
+        @pl.when(t == 6)
+        def _():
+            residual.start()
+
         for h in range(2):
-
-            @pl.when((t >= 4) & (half == h))
+            a = along[h]
+
+            @pl.when((t >= 2) & (t < 14) & (half == h))
             def _():
-                a = along[h]
                 line_wait(h, yy, (a + off) % 4)
 
-                @pl.when(t // 2 == 2)
+                @pl.when(q == 1)
                 def _():
                     send_line(h, y, (a + 3) % 4, (a + 1) % 4)
 
-                @pl.when(t // 2 == 3)
+                @pl.when(q == 2)
                 def _():
-                    send_line(h, y2, (a + 1) % 4, (a + 3) % 4)
-
-        @pl.when(t == 10)
-        def _():
-            residual.start()
+                    send_line(h, (y + 1) % 2, (a + 1) % 4, (a + 3) % 4)
 
     ss, pp = (s0, s1), (p0, p1)
-    TILE, CHUNK, STEPS = 256, 32, 8
+    TILE, STEPS = 256, 8
     ones = jnp.where(lane == 0, 1.0, 0.0).astype(BF16)
 
     def scores_rhs(bases, gl):
@@ -344,29 +384,40 @@
 
     def send_unit(t):
         half, yy, off = order(t)
-
-        @pl.when(t >= 0)
+        base = base_of(t)
+        line = half * 2 + yy
+        k = jnp.where(off == 2, 2, off // 2)
+        to = (s, device(half, y, (pick(half, along) + off) % 4, pick(half, within)))
+
+        @pl.when((t >= 0) & (off != 0))
         def _():
-            for w in range(4):
-                send_block_out(half, bases_of(t)[0], w, yy, (pick(half, along) + off) % 4)
+            blocks = pl.ds(base, 4)
+            send_to(po.at[blocks], r1.at[line, k], u1s, u1r.at[line, k], to)
+            send_to(pa.at[blocks], a1.at[line, k], b1s, b1r.at[line, k], to)
 
     def unit(accs, t, c):
         arrived(t)
+        send_unit(t - 2)
+
+        @pl.when(t == 14)
+        def _():
+            own_block(accs)
 
         @pl.when(t == 15)
         def _():
-            own_block(accs)
+            def both(half, c2):
+                join(half, 0)
+                return c2
+
+            lax.fori_loop(0, 2, both, 0)
 
         tb = jnp.maximum(t - 1, 0)
-        new = lambda gl: (bases_of(t), t % 2, t % 2, gl)
-        old = lambda gl: (bases_of(tb), tb % 2, (t + 1) % 2, gl)
+        new = lambda gl: ((base_of(t),), t % 2, t % 2, gl)
+        old = lambda gl: ((base_of(tb),), tb % 2, (t + 1) % 2, gl)
         todo = step(accs, new(0), old(3), old(2), ())
         todo = step(accs, new(1), new(0), old(3), todo)
-        for last in todo:
-            last()
-        pack_notes(bases_of(tb), (t + 1) % 2)
-        send_unit(t - 1)
-        todo = step(accs, new(2), new(1), new(0), ())
+        todo = step(accs, new(2), new(1), new(0), todo)
+        pack_notes((base_of(tb),), (t + 1) % 2)
         todo = step(accs, new(3), new(2), new(1), todo)
         for last in todo:
             last()
@@ -381,7 +432,7 @@
 
     def units(*accs):
         lax.fori_loop(0, 16, functools.partial(unit, accs), 0)
-        bases, value = bases_of(15), accs[3]
+        bases, value = (base_of(15),), accs[3]
         m, total = jnp.max(mx[1], axis=0, keepdims=True), None
         for j in range(STEPS):
             values_push(j, 0)
@@ -396,8 +447,9 @@
 
     shapes = ((0, UROWS), (0, UROWS), (1, UROWS), (1, HD), (1, HD))
     pl.run_scoped(units, *(pltpu.ACC(one)((size, 2 * HD), F32) for one, size in shapes))
-    pack_notes(bases_of(15), 1)
-    send_unit(15)
+    join(0, 1)
+    pack_notes((base_of(15),), 1)
+    join(1, 1)
 
     pltpu.make_async_copy(ra, ra, b2r).wait()
     cols = lax.broadcasted_iota(jnp.int32, (QB, HD), 1)
@@ -422,28 +474,17 @@
     residual.wait_recv()
 
     for half in range(2):
-        parts = rp.at[pl.ds(half * NKV, NKV)]
+        parts = rp.at[pl.ds(half * SLOTS, SLOTS)]
         pltpu.make_async_copy(parts, parts, u2r.at[half]).wait()
-        pltpu.make_async_copy(rb.at[half], rb.at[half], v2r.at[half]).wait()
-
-        def add(n, acc):
-            factors = ra[pl.ds(half * SLOTS + n * 16, 16)].reshape(HD, HD).T
-            for i in range(16):
-                part = rp[half * NKV + n * 16 + i]
-                acc = tuple(
-                    acc[gl]
-                    + part[gl].astype(jnp.int32).astype(F32) * factors[0:ROWS, i * 8 + gl : i * 8 + gl + 1]
-                    for gl in range(GH)
-                )
-            return acc
-
-        acc = lax.fori_loop(0, 2, add, tuple(jnp.zeros((ROWS, HD), F32) for _ in range(GH)))
-        rows = ra[half * SLOTS + NKV : (half + 1) * SLOTS].reshape(32, HD)
-        factors = jnp.concatenate([rows, jnp.zeros((HD - 32, HD), F32)], axis=0).T
-        acc = [
-            acc[gl] + rb[half, gl].astype(jnp.int32).astype(F32) * factors[0:ROWS, gl * 9 : gl * 9 + 1]
-            for gl in range(GH)
-        ]
+
+        f = ra[half * SLOTS : (half + 1) * SLOTS].reshape(SLOTS * 8, HD)
+        factors = jnp.concatenate([f, jnp.zeros((HD - SLOTS * 8, HD), F32)], axis=0).T
+        acc = [None] * GH
+        for i in range(SLOTS):
+            for gl in range(GH):
+                part = rp[half * SLOTS + i, gl].astype(jnp.int32).astype(F32)
+                part = part * factors[0:ROWS, i * 8 + gl : i * 8 + gl + 1]
+                acc[gl] = part if i == 0 else acc[gl] + part
         for gl in range(GH):
             for h in range(8):
                 c0 = ((half * GH + gl) * 8 + h) * HD
@@ -459,7 +500,7 @@
     pltpu.make_async_copy(blocks, blocks, g2s).wait()
     blocks = ga.at[pl.ds(0, 48), 0, ROWS:BLK]
     pltpu.make_async_copy(blocks, blocks, g3s).wait()
-    for ref, sem in ((po, u2s), (bp, v2s), (ra, b2s)):
+    for ref, sem in ((po.at[pl.ds(0, 48)], u1s), (pa.at[pl.ds(0, 48)], b1s), (po2, u2s), (pa2, b2s)):
         pltpu.make_async_copy(ref, ref, sem).wait()
 
 
@@ -480,10 +521,13 @@
             pltpu.VMEM((CTX, HD), BF16),
             pltpu.VMEM((2 * NKV, GH, ROWS, HD), I16),
             pltpu.VMEM((2 * NKV, 8, HD), F32),
+            pltpu.VMEM((4, 3, 4, GH, ROWS, HD), I16),
+            pltpu.VMEM((4, 3, 4, 8, HD), F32),
             pltpu.VMEM((2, 4, ROWS, HD), I16),
             pltpu.VMEM((2, 4, 8, HD), F32),
-            pltpu.VMEM((2 * NKV, GH, ROWS, HD), I16),
-            pltpu.VMEM((2, GH, ROWS, HD), I16),
+            pltpu.VMEM((4, 4, GH, ROWS, HD), I16),
+            pltpu.VMEM((4, 4, 8, HD), F32),
+            pltpu.VMEM((2 * SLOTS, GH, ROWS, HD), I16),
             pltpu.VMEM((2 * SLOTS, 8, HD), F32),
             pltpu.VMEM((QB, HQ * HD), F32),
             pltpu.VMEM((QB, HQ * HD), F32),
@@ -504,7 +548,9 @@
             dma,
             dma((2, 8)),
             dma,
-            dma((2,)),
+            dma((4, 3)),
+            dma,
+            dma((4, 3)),
             dma,
             dma((2,)),
             dma,

time: 111 us -> 111 us (level)
  no operation moved by 1% of the time
where the time goes in v2:
time: 111 us
  Pallas kernels  107 us (96%)
  local copies, waits for them, and re-layouts  2.95 us (3%)
  between operations  1.29 us (1%)
    pallas_call x1, Pallas kernels, per_device(): pl.pallas_call(kernel, out_shape=(jax.ShapeDtypeStruct((QB, HQ * HD), F32...  107 us
    unnamed x2, local copies, waits for them, and re-layouts  2.95 us

profile of v2, /device:TPU:1, one launch (start us, length us, event | category | flops | bytes accessed | tf_op | source)
XLA Modules:
  0.0 110.8 jit_solution(14249951280083386781)
XLA Ops:
  1.3 106.6 %shard_map.86 = (f32[8,8192]{1,0:T(8,128)}, f32[8,64]{1,0:T(8,128)}) custom-call(s32[1,1]{1,0:T(1,128)S(6)} %copy.11.len_ref, bf16[8,8192]{1,0:T(8,128)(2,1)} %bitcast.12, bf16[8,1024]{1,0:T(8,128)(2,1)} %bitcast.14, bf16[8,1024]{1,0:T(8,128)(2,1)} %bitcast.15, bf16[8,8192]{1,0:T(8,128)(2,1)} %bitcast.13, bf16[2048,1024]{1,0:T(8,128)(2,1)} %bitcast.10, ...), custom_call_target="tpu_custom_call" | custom-call | flops 17179869184 | bytes 12582912 | tf_op jit(solution)/shard_map/pallas_call | solution.py:511
  107.9 1.7 %copy.12 = f32[1,8,8192]{2,1,0:T(8,128)} copy(f32[1,8,8192]{2,1,0:T(8,128)} %bitcast.8) | data formatting | bytes 524288
  109.5 1.3 %copy.13 = f32[1,8,64]{2,1,0:T(8,128)} copy(f32[1,8,64]{2,1,0:T(8,128)} %bitcast.9) | data formatting | bytes 4096
